TPU v7x, 32 devices: a whole 2x2x4 slice. The times are simulated.
32 devices in a mesh: fsdp: 8 (over y, x, core), seq: 4 (over z).
Axes of the slice: x: 2, y: 2, z: 4, core: 2. Of those that a mesh axis runs over, the one named last changes fastest.
Arguments:
- layer_input: bfloat16 [8, 2, 1024, 768], P('fsdp', None, 'seq'), may hold values from -6 to 6
- segment_ids: int32 [8, 2, 1024], P('fsdp'), may hold values from 0 to 2, as said below
- gain_in: bfloat16 [768], P('fsdp'), may hold values from 0.5 to 1.5
- in_weight: bfloat16 [768, 3352], P('fsdp'), may hold values from -0.21875 to 0.21875
- conv_weight: bfloat16 [1792, 4], P('fsdp'), may hold values from -3 to 3
- conv_bias: bfloat16 [1792], P('fsdp'), may hold values from -0.5 to 0.5
- dt_bias: bfloat16 [24], replicated, may hold values from -7 to -2.296875
- a_log: bfloat16 [24], replicated, may hold values from 0 to 2.765625
- skip_gain: bfloat16 [24], replicated, may hold values from 0.5 to 1.5
- gain_out: bfloat16 [1536], P('fsdp'), may hold values from 0.5 to 1.5
- out_weight: bfloat16 [1536, 768], P('fsdp'), may hold values from -0.15625 to 0.15625
- cotangent: bfloat16 [8, 2, 1024, 768], P('fsdp', None, 'seq'), may hold values from -6 to 6
Outputs:
- layer_output: bfloat16 [8, 2, 1024, 768], P('fsdp', None, 'seq')
- input_grad: float32 [8, 2, 1024, 768], P('fsdp', None, 'seq')
- grad_gain_in: float32 [768], P('fsdp')
- grad_in_weight: float32 [768, 3352], P('fsdp')
- grad_conv_weight: float32 [1792, 4], P('fsdp')
- grad_conv_bias: float32 [1792], P('fsdp')
- grad_dt_bias: float32 [24], replicated
- grad_a_log: float32 [24], replicated
- grad_skip_gain: float32 [24], replicated
- grad_gain_out: float32 [1536], P('fsdp')
- grad_out_weight: float32 [1536, 768], P('fsdp')
Inputs may be any that keep to these rules, and one draw needn't show every extreme that they name: `segment_ids`: along each sequence the segment numbers start at 0 and never fall; segment 1 begins within the first 256 positions and segment 2 within the last 256, so all three are present.
All inputs are finite; a program needn't handle non-finite values.
Results may differ from a plain program's by a relative error of at most 0.012.
Values may be sent and summed in bfloat16 or wider, within the bound.
No kernel may reach another device: no remote copies, remote signals or barrier semaphores. Data moves between devices by JAX's collectives and lax.ppermute only.
A program may use at most 128 MiB of HBM per device.

v0:
```python
from functools import partial

import jax
import jax.numpy as jnp
from jax import lax
from jax.sharding import PartitionSpec as P

INNER = 1536
HEADDIM = 64
SPAN = 256


EPS_NORM = 1e-05
HIGHEST_PRECISION = lax.Precision.HIGHEST


def front_norm(tokens_in, gain_vec):
    meansq = jnp.mean(tokens_in * tokens_in, axis=-1, keepdims=True)
    return tokens_in * lax.rsqrt(meansq + EPS_NORM) * gain_vec


def gated_norm(mixed_rows, gating, gain_vec):
    gated = mixed_rows * jax.nn.silu(gating)
    meansq = jnp.mean(gated * gated, axis=-1, keepdims=True)
    return gated * lax.rsqrt(meansq + EPS_NORM) * gain_vec


def causal_conv(values, kernel_w, bias_vec, seg_ids):
    length = values.shape[0]
    tap_count = kernel_w.shape[1]
    running = bias_vec[None, :] + kernel_w[:, tap_count - 1][None, :] * values
    for offset in range(1, tap_count):
        shifted = jnp.concatenate(
            [jnp.zeros((offset, values.shape[1]), values.dtype), values[: length - offset]], 0
        )
        earlier = jnp.concatenate(
            [jnp.full((offset,), -1, jnp.int32), seg_ids[: length - offset]], 0
        )
        keep_mask = (earlier == seg_ids).astype(values.dtype)
        running = (
            running + kernel_w[:, tap_count - 1 - offset][None, :] * shifted * keep_mask[:, None]
        )
    return running


def scan_blocks(x_heads, step_size, rates, b_mat, c_mat, seg_ids):
    length, head_count, head_width = x_heads.shape
    state_size = b_mat.shape[1]
    block_count = length // SPAN
    x_blocks = x_heads.reshape(block_count, SPAN, head_count, head_width)
    dt_blocks = step_size.reshape(block_count, SPAN, head_count)
    b_blocks = b_mat.reshape(block_count, SPAN, state_size)
    c_blocks = c_mat.reshape(block_count, SPAN, state_size)
    s_blocks = seg_ids.reshape(block_count, SPAN)
    rows_iota = lax.broadcasted_iota(jnp.int32, (SPAN, SPAN), 0)
    cols_iota = lax.broadcasted_iota(jnp.int32, (SPAN, SPAN), 1)

    def block_step(carry, item):
        carried_state, last_seg = carry
        x_blk, dt_blk, b_blk, c_blk, seg_blk = item
        logs = jnp.cumsum(dt_blk * rates[None, :], axis=0)
        inside = (rows_iota >= cols_iota) & (seg_blk[:, None] == seg_blk[None, :])
        logs_t = logs.T
        diffs = jnp.where(inside[None], logs_t[:, :, None] - logs_t[:, None, :], -jnp.inf)
        scores = jnp.dot(c_blk, b_blk.T, precision=HIGHEST_PRECISION)
        weights = scores[None] * jnp.exp(diffs) * dt_blk.T[:, None, :]
        y_inner = jnp.einsum("hij,jhp->ihp", weights, x_blk, precision=HIGHEST_PRECISION)
        carried = (seg_blk == last_seg).astype(jnp.float32)
        y_outer = jnp.einsum("in,hpn->ihp", c_blk, carried_state, precision=HIGHEST_PRECISION)
        y_outer = y_outer * (jnp.exp(logs) * carried[:, None])[:, :, None]
        tail_w = (
            jnp.exp(logs[-1][None, :] - logs)
            * dt_blk
            * (seg_blk == seg_blk[-1]).astype(jnp.float32)[:, None]
        )
        fresh = jnp.einsum("jh,jhp,jn->hpn", tail_w, x_blk, b_blk, precision=HIGHEST_PRECISION)
        keep_flag = (seg_blk[-1] == last_seg).astype(jnp.float32)
        new_state = fresh + (jnp.exp(logs[-1]) * keep_flag)[:, None, None] * carried_state
        return ((new_state, seg_blk[-1]), y_inner + y_outer)

    start_state = jnp.zeros((head_count, head_width, state_size), jnp.float32)
    carry_out, y_blocks = lax.scan(
        jax.checkpoint(block_step),
        (start_state, jnp.int32(-1)),
        (x_blocks, dt_blocks, b_blocks, c_blocks, s_blocks),
    )
    return y_blocks.reshape(length, head_count, head_width)


def mixer_heads(
    seg_ids, x_pre, bc_pre, dt_raw, conv_wx, conv_bx, conv_wbc, conv_bbc, dt_bias, a_log, skip_gain
):
    x_act = jax.nn.silu(causal_conv(x_pre, conv_wx, conv_bx, seg_ids))
    bc_act = jax.nn.silu(causal_conv(bc_pre, conv_wbc, conv_bbc, seg_ids))
    state_size = bc_pre.shape[1] // 2
    head_count = dt_raw.shape[1]
    x_heads = x_act.reshape(x_act.shape[0], head_count, x_act.shape[1] // head_count)
    step_size = jax.nn.softplus(dt_raw + dt_bias[None, :])
    rates = -jnp.exp(a_log)
    scanned = scan_blocks(
        x_heads, step_size, rates, bc_act[:, :state_size], bc_act[:, state_size:], seg_ids
    )
    return scanned + skip_gain[None, :, None] * x_heads


def on_device(
    layer_input,
    segment_ids,
    gain_in,
    in_weight,
    conv_weight,
    conv_bias,
    dt_bias,
    a_log,
    skip_gain,
    gain_out,
    out_weight,
    cotangent,
):
    gain_whole, in_whole = (
        lax.all_gather(gain_in, "fsdp", axis=0, tiled=True),
        lax.all_gather(in_weight, "fsdp", axis=0, tiled=True),
    )
    convw_whole, convb_whole, gout_whole, out_whole = (
        lax.all_gather(conv_weight, "fsdp", axis=0, tiled=True),
        lax.all_gather(conv_bias, "fsdp", axis=0, tiled=True),
        lax.all_gather(gain_out, "fsdp", axis=0, tiled=True),
        lax.all_gather(out_weight, "fsdp", axis=0, tiled=True),
    )
    micro_count = layer_input.shape[1]
    part_len = layer_input.shape[2]
    head_count = dt_bias.shape[0]
    conv_chans = convw_whole.shape[0]
    tap_count = convw_whole.shape[1]
    local_heads = head_count // lax.axis_size("seq")
    head_start = lax.axis_index("seq") * local_heads
    chan_start = head_start * HEADDIM
    local_chans = local_heads * HEADDIM
    gain_front = gain_whole.astype(jnp.float32)
    gain_back = gout_whole.astype(jnp.float32)
    convw_float = convw_whole.astype(jnp.float32)
    convb_float = convb_whole.astype(jnp.float32)
    params_local = (
        lax.dynamic_slice_in_dim(convw_float, chan_start, local_chans, 0),
        lax.dynamic_slice_in_dim(convb_float, chan_start, local_chans, 0),
        convw_float[INNER:],
        convb_float[INNER:],
        lax.dynamic_slice_in_dim(dt_bias.astype(jnp.float32), head_start, local_heads, 0),
        lax.dynamic_slice_in_dim(a_log.astype(jnp.float32), head_start, local_heads, 0),
        lax.dynamic_slice_in_dim(skip_gain.astype(jnp.float32), head_start, local_heads, 0),
    )
    grad_front_gain = jnp.zeros_like(gain_front)
    grad_in_mat = jnp.zeros(in_whole.shape, jnp.float32)
    grad_back_gain = jnp.zeros_like(gain_back)
    grad_out_mat = jnp.zeros(out_whole.shape, jnp.float32)
    grad_local = tuple((jnp.zeros_like(param_val) for param_val in params_local))
    outputs_list = []
    input_grads = []
    for micro_idx in range(micro_count):
        tokens_in = layer_input[0, micro_idx].astype(jnp.float32)
        seg_ids = segment_ids[0, micro_idx]
        normed_float, front_pull = jax.vjp(front_norm, tokens_in, gain_front)
        normed = normed_float.astype(jnp.bfloat16)
        projected = jnp.dot(normed, in_whole, preferred_element_type=jnp.float32)
        gating = projected[:, :INNER]
        x_send = (
            projected[:, INNER : 2 * INNER]
            .astype(jnp.bfloat16)
            .reshape(part_len, head_count, HEADDIM)
        )
        bc_send = projected[:, 2 * INNER : INNER + conv_chans].astype(jnp.bfloat16)
        dt_send = projected[:, INNER + conv_chans :].astype(jnp.bfloat16)
        bc_whole = lax.all_gather(bc_send, "seq", axis=0, tiled=True)
        x_group, dt_group = (
            lax.all_to_all(x_send, "seq", split_axis=1, concat_axis=0, tiled=True),
            lax.all_to_all(dt_send, "seq", split_axis=1, concat_axis=0, tiled=True),
        )
        seq_len = x_group.shape[0]
        mixed_float, mixer_pull = jax.vjp(
            partial(mixer_heads, seg_ids),
            x_group.reshape(seq_len, local_chans).astype(jnp.float32),
            bc_whole.astype(jnp.float32),
            dt_group.astype(jnp.float32),
            params_local[0],
            params_local[1],
            params_local[2],
            params_local[3],
            params_local[4],
            params_local[5],
            params_local[6],
        )
        mixed_tokens = lax.all_to_all(
            mixed_float.astype(jnp.bfloat16), "seq", split_axis=0, concat_axis=1, tiled=True
        )
        mixed_rows = mixed_tokens.reshape(part_len, INNER).astype(jnp.float32)
        outnorm_float, back_pull = jax.vjp(gated_norm, mixed_rows, gating, gain_back)
        out_normed = outnorm_float.astype(jnp.bfloat16)
        result = tokens_in + jnp.dot(out_normed, out_whole, preferred_element_type=jnp.float32)
        outputs_list.append(result.astype(jnp.bfloat16))
        cot_rows = cotangent[0, micro_idx]
        grad_out_mat = grad_out_mat + jnp.dot(
            out_normed.T, cot_rows, preferred_element_type=jnp.float32
        )
        grad_outnorm = jnp.dot(cot_rows, out_whole.T, preferred_element_type=jnp.float32)
        grad_mixed, grad_gating, grad_gainback = back_pull(grad_outnorm)
        grad_back_gain = grad_back_gain + grad_gainback
        grad_group = lax.all_to_all(
            grad_mixed.astype(jnp.bfloat16).reshape(part_len, head_count, HEADDIM),
            "seq",
            split_axis=1,
            concat_axis=0,
            tiled=True,
        )
        mixer_grads = mixer_pull(grad_group.astype(jnp.float32))
        grad_local = tuple((before + added for before, added in zip(grad_local, mixer_grads[3:])))
        grad_xtok, grad_dttok = (
            lax.all_to_all(
                mixer_grads[0].astype(jnp.bfloat16).reshape(seq_len, local_heads, HEADDIM),
                "seq",
                split_axis=0,
                concat_axis=1,
                tiled=True,
            ),
            lax.all_to_all(
                mixer_grads[2].astype(jnp.bfloat16), "seq", split_axis=0, concat_axis=1, tiled=True
            ),
        )
        grad_bctok = lax.psum_scatter(
            mixer_grads[1].astype(jnp.bfloat16), "seq", scatter_dimension=0, tiled=True
        )
        grad_proj = jnp.concatenate(
            [
                grad_gating.astype(jnp.bfloat16),
                grad_xtok.reshape(part_len, INNER),
                grad_bctok,
                grad_dttok,
            ],
            axis=1,
        )
        grad_in_mat = grad_in_mat + jnp.dot(normed.T, grad_proj, preferred_element_type=jnp.float32)
        grad_normed = jnp.dot(grad_proj, in_whole.T, preferred_element_type=jnp.float32)
        grad_tokens, grad_gainfront = front_pull(grad_normed)
        grad_front_gain = grad_front_gain + grad_gainfront
        input_grads.append(cot_rows.astype(jnp.float32) + grad_tokens)
    layer_output = jnp.stack(outputs_list, 0)[None]
    input_grad = jnp.stack(input_grads, 0)[None]
    grad_convw = jnp.concatenate(
        [
            lax.dynamic_update_slice_in_dim(
                jnp.zeros((INNER, tap_count), jnp.float32), grad_local[0], chan_start, 0
            ),
            grad_local[2],
        ],
        0,
    )
    grad_convb = jnp.concatenate(
        [
            lax.dynamic_update_slice_in_dim(
                jnp.zeros((INNER,), jnp.float32), grad_local[1], chan_start, 0
            ),
            grad_local[3],
        ],
        0,
    )
    zero_heads = jnp.zeros((head_count,), jnp.float32)
    grad_dtb = lax.dynamic_update_slice_in_dim(zero_heads, grad_local[4], head_start, 0)
    grad_alog = lax.dynamic_update_slice_in_dim(zero_heads, grad_local[5], head_start, 0)
    grad_skip = lax.dynamic_update_slice_in_dim(zero_heads, grad_local[6], head_start, 0)
    partials = (
        lax.psum_scatter(grad_front_gain, "fsdp", scatter_dimension=0, tiled=True),
        lax.psum_scatter(grad_in_mat, "fsdp", scatter_dimension=0, tiled=True),
        lax.psum_scatter(grad_convw, "fsdp", scatter_dimension=0, tiled=True),
        lax.psum_scatter(grad_convb, "fsdp", scatter_dimension=0, tiled=True),
        lax.psum_scatter(grad_back_gain, "fsdp", scatter_dimension=0, tiled=True),
        lax.psum_scatter(grad_out_mat, "fsdp", scatter_dimension=0, tiled=True),
    )
    shares = lax.psum(
        (partials[0], partials[1], partials[2], partials[3], partials[4], partials[5]), "seq"
    )
    head_sums = lax.psum((grad_dtb, grad_alog, grad_skip), ("fsdp", "seq"))
    return (
        layer_output,
        input_grad,
        shares[0],
        shares[1],
        shares[2],
        shares[3],
        head_sums[0],
        head_sums[1],
        head_sums[2],
        shares[4],
        shares[5],
    )


def solution(mesh):
    placed = (
        P("fsdp", None, "seq", None),
        P("fsdp", None, None),
        P("fsdp"),
        P("fsdp", None),
        P("fsdp", None),
        P("fsdp"),
        P(),
        P(),
        P(),
        P("fsdp"),
        P("fsdp", None),
        P("fsdp", None, "seq", None),
    )
    return jax.shard_map(
        on_device,
        mesh=mesh,
        in_specs=placed,
        out_specs=(
            P("fsdp", None, "seq", None),
            P("fsdp", None, "seq", None),
            P("fsdp"),
            P("fsdp", None),
            P("fsdp", None),
            P("fsdp"),
            P(),
            P(),
            P(),
            P("fsdp"),
            P("fsdp", None),
        ),
        check_vma=False,
    )
```

profile of v0, /device:TPU:0, one launch (start us, length us, event | category | flops | bytes accessed | tf_op | source)
XLA Modules:
  0.0 1588.4 jit_solution(5554178233122813119)
XLA Ops:
  16.9 26.0 %all-reduce.62 = (bf16[768]{0:T(1024)(128)(2,1)S(1)}, bf16[1792]{0:T(1024)(128)(2,1)S(1)}, bf16[1536]{0:T(1024)(128)(2,1)}) all-reduce(bf16[768]{0:T(1024)(128)(2,1)S(1)} %dynamic-update-slice, bf16[1792]{0:T(1024)(128)(2,1)S(1)} %dynamic-update-slice.1, ...), channel_id=1, replica_groups=mesh['fsdp'=8,'seq'=4] {'fsdp'}, use_global_device_ids=true, to_apply=%add.52 | all-reduce | flops 4096 | bytes 16384
  94.5 24.8 %all_gather.28 = bf16[1024,256]{0,1:T(8,128)(2,1)S(1)} all-gather(bf16[256,256]{0,1:T(8,128)(2,1)S(1)} %slice.426), channel_id=1, replica_groups=mesh['fsdp'=8,'seq'=4] {'seq'}, dimensions={0}, use_global_device_ids=true | all-gather | bytes 655360 | tf_op jit(solution)/shard_map/all_gather | solution.py:173
  121.8 16.2 %all_gather.31 = bf16[1024,256]{0,1:T(8,128)(2,1)S(1)} all-gather(bf16[256,256]{0,1:T(8,128)(2,1)S(1)} %slice.441), channel_id=1, replica_groups=mesh['fsdp'=8,'seq'=4] {'seq'}, dimensions={0}, use_global_device_ids=true | all-gather | bytes 655360 | tf_op jit(solution)/shard_map/all_gather | solution.py:173
  178.1 135.3 %while.91 = (s32[]{:T(128)}, f32[6,64,128]{2,1,0:T(8,128)S(1)}, s32[]{:T(128)}, f32[4,256,6,64]{1,0,3,2:T(4,128)}, f32[4,6,64,128]{3,2,1,0:T(8,128)}, /*index=5*...) while((s32[]{:T(128)}, f32[6,64,128]{2,1,0:T(8,128)S(1)}, ...), condition=%wide.region_10.12_spmd.clone, body=%wide.region_7.11_spmd.clone.sunk | while | flops 707158528 | bytes 5855851 | solution.py:82
  197.9 9.5 dynamic_update_slice.172
  231.7 9.5 dynamic_update_slice.172
  265.5 9.5 dynamic_update_slice.172
  299.3 9.5 dynamic_update_slice.172
  322.1 112.8 %while.90 = (s32[]{:T(128)}, f32[6,64,128]{2,1,0:T(8,128)S(1)}, s32[]{:T(128)}, f32[4,256,6,64]{1,0,3,2:T(4,128)}, f32[4,6,64,128]{3,2,1,0:T(8,128)}, /*index=5*...) while((s32[]{:T(128)}, f32[6,64,128]{2,1,0:T(8,128)S(1)}, ...), condition=%wide.region_4.6_spmd.clone, body=%wide.region_1.5_spmd.clone.sunk | while | flops 707158528 | bytes 5849555 | solution.py:82
  335.8 9.5 dynamic_update_slice.169
  364.0 9.5 dynamic_update_slice.169
  392.2 9.5 dynamic_update_slice.169
  420.4 9.5 dynamic_update_slice.169
  530.6 11.1 all-to-all-done.9
  552.1 335.2 %while.93 = (s32[]{:T(128)}, f32[6]{0:T(128)}, f32[6,64,128]{2,1,0:T(8,128)}, f32[4,256,6,64]{1,0,3,2:T(4,128)}, f32[4,256,6]{1,2,0:T(8,128)}, /*index=5*/f32[4,...) while((s32[]{:T(128)}, f32[6]{0:T(128)}, ...), condition=%wide.region_43.45_spmd.clone, body=%wide.region_30.44_spmd.clone.sunk | while | flops 1669388800 | bytes 21708672 | solution.py:82
  621.0 9.6 dynamic_update_slice.181
  704.5 9.6 dynamic_update_slice.181
  788.7 9.6 dynamic_update_slice.181
  872.8 9.6 dynamic_update_slice.181
  899.7 334.3 %while.92 = (s32[]{:T(128)}, f32[6]{0:T(128)}, f32[6,64,128]{2,1,0:T(8,128)}, f32[4,256,6,64]{1,0,3,2:T(4,128)}, f32[4,256,6]{1,2,0:T(8,128)}, /*index=5*/f32[4,...) while((s32[]{:T(128)}, f32[6]{0:T(128)}, ...), condition=%wide.region_26.28_spmd.clone, body=%wide.region_13.27_spmd.clone.sunk | while | flops 1669388800 | bytes 21708672 | solution.py:82
  968.4 9.5 dynamic_update_slice.177
  1051.7 9.5 dynamic_update_slice.177
  1135.6 9.5 dynamic_update_slice.177
  1297.7 10.5 all_to_all.148
  1325.4 11.2 all-to-all-done.7
  1347.5 9.7 all-to-all-done.10
  1369.4 10.1 convolution_add_fusion.8
  1387.1 37.6 %all-reduce.58 = (f32[24]{0:T(128)}, f32[24]{0:T(128)}, f32[24]{0:T(128)}) all-reduce(f32[24]{0:T(128)S(1)} %add_dynamic-update-slice_fusion.3, f32[24]{0:T(128)S(1)} %multiply_dynamic-update-slice_fusion, f32[24]{0:T(128)S(1)} %add_dynamic-update-slice_fusion.2), channel_id=1, replica_groups=mesh['fsdp'=8,'seq'=4] {'fsdp','seq'}, use_global_device_ids=true, to_apply=%region_78.80 | all-reduce | flops 72 | bytes 576 | tf_op jit(solution)/shard_map/psum | solution.py:280
  1426.1 67.7 %reduce-scatter.12.cloned.1.call-done = f32[96,3352]{1,0:T(8,128)} async-done(((f32[768,3352]{1,0:T(8,128)}), f32[96,3352]{1,0:T(8,128)}) %reduce-scatter.12.cloned.1.call-update) | async-done | bytes 1287184 | tf_op jit(solution)/shard_map/reduce_scatter | solution.py:271
  1503.6 24.7 %all-reduce.59 = (f32[768]{0:T(1024)S(1)}, f32[1792]{0:T(1024)S(1)}, f32[1536]{0:T(1024)S(1)}) all-reduce(f32[768]{0:T(1024)S(1)} %add.448, f32[1792]{0:T(1024)S(1)} %pad_maximum_fusion.7, f32[1536]{0:T(1024)S(1)} %add.458), channel_id=4, replica_groups=mesh['fsdp'=8,'seq'=4] {'fsdp'}, use_global_device_ids=true, to_apply=%region_48.50.clone | all-reduce | flops 4096 | bytes 32768
  1528.5 12.4 all-reduce.60
  1544.1 33.9 %all-reduce.65.cloned.1.call-done = (f32[96,3352]{1,0:T(8,128)}, f32[192,768]{1,0:T(8,128)}) async-done(((f32[96,3352]{1,0:T(8,128)}, f32[192,768]{1,0:T(8,128)}), (f32[96,3352]{1,0:T(8,128)}, f32[192,768]{1,0:T(8,128)})) %all-reduce.65.cloned.1.call-update) | async-done | bytes 1877008 | tf_op jit(solution)/shard_map/psum | solution.py:277
  (1517 shorter events, 1106.4 us)
Async XLA Ops:
  7.2 35.7 %copy-start.22 = (bf16[1,2,256,768]{3,2,1,0:T(8,128)(2,1)S(1)}, bf16[1,2,256,768]{3,2,1,0:T(8,128)(2,1)}, u32[]{:S(2)}) copy-start(bf16[1,2,256,768]{3,2,1,0:T(8,128)(2,1)} %param.21) | copy-start | bytes 2359300
  7.2 36.0 %copy-start.175 = (bf16[224,4]{0,1:T(4,128)(2,1)S(1)}, bf16[224,4]{0,1:T(4,128)(2,1)}, u32[]{:S(2)}) copy-start(bf16[224,4]{0,1:T(4,128)(2,1)} %param.25) | copy-start | bytes 5380
  7.2 47.1 %all-gather.4.cloned.1.call-start = ((), (), s32[]{:S(2)}) async-start(), calls=%async_computation.17 | async-start | bytes 5971968 | tf_op jit(solution)/shard_map/all_gather | solution.py:122
  7.9 470.6 %all-gather.6.cloned.1.call-start = ((), (), s32[]{:S(2)}) async-start(), calls=%async_computation.18 | async-start | bytes 2654208 | tf_op jit(solution)/shard_map/all_gather | solution.py:128
  61.5 13.0 all-to-all-start
  74.5 10.8 all-to-all-start.3
  85.3 56.1 %all-to-all-start.1 = ((bf16[256,24,64]{0,2,1:T(8,128)(2,1)}), bf16[256,24,64]{0,2,1:T(8,128)(2,1)}, u32[]{:S(2)}, u32[]{:S(2)}) async-start(bf16[256,24,64]{0,2,1:T(8,128)(2,1)} %bitcast.9), calls=%async_computation.1 | async-start | bytes 1572864 | tf_op jit(solution)/shard_map/all_to_all | solution.py:175
  91.7 72.6 %copy-start.122 = (f32[1024]{0:T(1024)}, f32[1024]{0:T(1024)S(1)}, u32[]{:S(2)}) copy-start(f32[1024]{0:T(1024)S(1)} %get-tuple-element.1950) | copy-start | bytes 12292
  91.7 72.6 %copy-start.124 = (f32[1024]{0:T(1024)}, f32[1024]{0:T(1024)S(1)}, u32[]{:S(2)}) copy-start(f32[1024]{0:T(1024)S(1)} %get-tuple-element.1952) | copy-start | bytes 12292
  92.4 72.0 %copy-start.126 = (f32[1024]{0:T(1024)}, f32[1024]{0:T(1024)S(1)}, u32[]{:S(2)}) copy-start(f32[1024]{0:T(1024)S(1)} %get-tuple-element.1953) | copy-start | bytes 12292
  92.4 72.0 %copy-start.128 = (f32[1024]{0:T(1024)}, f32[1024]{0:T(1024)S(1)}, u32[]{:S(2)}) copy-start(f32[1024]{0:T(1024)S(1)} %get-tuple-element.1955) | copy-start | bytes 12292
  141.4 20.2 %all-to-all-start.4 = ((bf16[256,24,64]{0,2,1:T(8,128)(2,1)}), bf16[256,24,64]{0,2,1:T(8,128)(2,1)}, u32[]{:S(2)}, u32[]{:S(2)}) async-start(bf16[256,24,64]{0,2,1:T(8,128)(2,1)} %bitcast.974), calls=%async_computation.4 | async-start | bytes 1572864 | tf_op jit(solution)/shard_map/all_to_all | solution.py:175
  453.5 20.8 %all-to-all-start.2 = ((bf16[4,2,49152]{2,1,0:T(2,128)(2,1)}), bf16[4,2,49152]{2,1,0:T(2,128)(2,1)}, u32[]{:S(2)}, u32[]{:S(2)}) async-start(bf16[4,2,49152]{2,1,0:T(2,128)(2,1)} %reshape.1081), calls=%async_computation.2 | async-start | bytes 1572864 | tf_op jit(solution)/shard_map/all_to_all | solution.py:192
  474.3 23.5 %all-to-all-start.5 = ((bf16[4,2,49152]{2,1,0:T(2,128)(2,1)}), bf16[4,2,49152]{2,1,0:T(2,128)(2,1)}, u32[]{:S(2)}, u32[]{:S(2)}) async-start(bf16[4,2,49152]{2,1,0:T(2,128)(2,1)} %reshape.1079), calls=%async_computation.5 | async-start | bytes 1572864 | tf_op jit(solution)/shard_map/all_to_all | solution.py:192
  478.5 47.6 %copy-start.91 = (f32[1536]{0:T(1024)}, f32[1536]{0:T(1024)S(1)}, u32[]{:S(2)}) copy-start(f32[1536]{0:T(1024)S(1)} %convert_element_type.366) | copy-start | bytes 18436
  519.2 22.6 %all-to-all-start.9 = ((bf16[256,24,64]{0,2,1:T(8,128)(2,1)}), bf16[256,24,64]{0,2,1:T(8,128)(2,1)}, u32[]{:S(2)}, u32[]{:S(2)}) async-start(bf16[256,24,64]{0,2,1:T(8,128)(2,1)} %bitcast.969), calls=%async_computation.10 | async-start | bytes 1572864 | tf_op jit(solution)/shard_map/all_to_all | solution.py:207
  541.7 350.8 %all-to-all-start.6 = ((bf16[256,24,64]{0,2,1:T(8,128)(2,1)}), bf16[256,24,64]{0,2,1:T(8,128)(2,1)}, u32[]{:S(2)}, u32[]{:S(2)}) async-start(bf16[256,24,64]{0,2,1:T(8,128)(2,1)} %bitcast.966), calls=%async_computation.6 | async-start | bytes 1572864 | tf_op jit(solution)/shard_map/all_to_all | solution.py:207
  545.9 816.1 %reduce-scatter.8.cloned.1.call-start = ((), (), s32[]{:S(2)}) async-start(), calls=%async_computation.19 | async-start | bytes 655360 | tf_op jit(solution)/shard_map/reduce_scatter | solution.py:228
  1268.1 101.3 %reduce-scatter.10.cloned.1.call-start = ((), (), s32[]{:S(2)}) async-start(), calls=%async_computation.20 | async-start | bytes 655360 | tf_op jit(solution)/shard_map/reduce_scatter | solution.py:228
  1282.5 142.5 %reduce-scatter.16.cloned.1.call-start = ((), (), s32[]{:S(2)}) async-start(), calls=%async_computation.23 | async-start | bytes 1032192
  1290.5 135.6 %reduce-scatter.14.cloned.1.call-start = ((), (), s32[]{:S(2)}) async-start(), calls=%async_computation.22 | async-start | bytes 5308416 | tf_op jit(solution)/shard_map/reduce_scatter | solution.py:275
  1308.1 8.8 all-to-all-start.11
  1317.0 19.6 %all-to-all-start.7 = ((bf16[4,2,49152]{2,1,0:T(2,128)(2,1)}), bf16[4,2,49152]{2,1,0:T(2,128)(2,1)}, u32[]{:S(2)}, u32[]{:S(2)}) async-start(bf16[4,2,49152]{2,1,0:T(2,128)(2,1)} %reshape.1085), calls=%async_computation.7 | async-start | bytes 1572864 | tf_op jit(solution)/shard_map/all_to_all | solution.py:217
  1336.5 20.6 %all-to-all-start.10 = ((bf16[4,2,49152]{2,1,0:T(2,128)(2,1)}), bf16[4,2,49152]{2,1,0:T(2,128)(2,1)S(1)}, u32[]{:S(2)}, u32[]{:S(2)}) async-start(bf16[4,2,49152]{2,1,0:T(2,128)(2,1)} %reshape.1083), calls=%async_computation.11 | async-start | bytes 1572864 | tf_op jit(solution)/shard_map/all_to_all | solution.py:217
  1340.0 153.8 %reduce-scatter.12.cloned.1.call-start = ((), (), s32[]{:S(2)}) async-start(), calls=%async_computation.21 | async-start | bytes 11943936 | tf_op jit(solution)/shard_map/reduce_scatter | solution.py:271
  1379.6 198.4 %all-reduce.65.cloned.1.call-start = ((), (), s32[]{:S(2)}) async-start(), calls=%async_computation.24 | async-start | bytes 3833856 | tf_op jit(solution)/shard_map/psum | solution.py:277
  1385.3 108.5 %copy-start.65 = (bf16[256,1536]{0,1:T(8,128)(2,1)S(1)}, bf16[256,1536]{0,1:T(8,128)(2,1)}, u32[]{:S(2)}) copy-start(bf16[256,1536]{0,1:T(8,128)(2,1)} %get-tuple-element.1937) | copy-start | bytes 2359300
  1385.4 108.5 %copy-start.69 = (bf16[256,4,6,64]{0,3,2,1:T(8,128)(2,1)S(1)}, bf16[256,4,6,64]{0,3,2,1:T(8,128)(2,1)}, u32[]{:S(2)}) copy-start(bf16[256,4,6,64]{0,3,2,1:T(8,128)(2,1)} %copy-done.68) | copy-start | bytes 2359300
  1385.4 108.5 %copy-start.118 = (bf16[256,256]{0,1:T(8,128)(2,1)S(1)}, bf16[256,256]{0,1:T(8,128)(2,1)}, u32[]{:S(2)}) copy-start(bf16[256,256]{0,1:T(8,128)(2,1)} %reduce-scatter.10.cloned.1.call-done) | copy-start | bytes 393220
  1498.2 42.7 %copy-start.166 = (f32[256]{0:T(256)S(1)}, f32[256]{0:T(256)}, u32[]{:S(2)}) copy-start(f32[256]{0:T(256)} %copy-done.165) | copy-start | bytes 3076
  1498.2 42.7 %copy-start.168 = (f32[256]{0:T(256)S(1)}, f32[256]{0:T(256)}, u32[]{:S(2)}) copy-start(f32[256]{0:T(256)} %copy-done.167) | copy-start | bytes 3076
  1498.2 42.7 %copy-start.42 = (bf16[1,2,256,768]{3,2,1,0:T(8,128)(2,1)S(1)}, bf16[1,2,256,768]{3,2,1,0:T(8,128)(2,1)}, u32[]{:S(2)}) copy-start(bf16[1,2,256,768]{3,2,1,0:T(8,128)(2,1)} %param.32) | copy-start | bytes 2359300
  (319 other events, 1401.2 us)
Sparse Core Ops, SparseCore 0:
  9.9 44.3 all-gather.3
  56.2 28.9 all-gather.5
  1268.2 22.0 reduce-scatter.7
  1293.0 20.0 reduce-scatter.9
  1316.7 33.5 reduce-scatter.15
  1353.6 54.2 reduce-scatter.13
  1411.7 82.0 reduce-scatter.11
  1496.4 81.5 all-reduce.64
where the time goes:
time: 1610 us; the launch traced here: 1590 us
  local copies, waits for them, and re-layouts  554 us (34%)
  other arithmetic  366 us (23%)
  matrix products  264 us (16%)
  blocking collectives  161 us (10%)
  waiting for transfers between devices  151 us (9%)
  starting transfers between devices  49.5 us (3%)
  loops' own time  22.9 us (1%)
  between operations  20.1 us (1%)
    dynamic_update_slice x40, local copies, waits for them, and re-layouts, scan_blocks(): lax.scan(jax.checkpoint(block_step), (start_state, jnp.int32(-1)), (x_blo...  181 us
    another operation x64, other arithmetic  144 us
    another operation x129, local copies, waits for them, and re-layouts  103 us
    dot_general x24, matrix products, block_step(): jnp.einsum('hij,jhp->ihp', weights, x_blk, precision=HIGHEST_PRECISION)  74.7 us
    reduce_scatter x1, waiting for transfers between devices, on_device(): lax.psum_scatter(grad_in_mat, 'fsdp', scatter_dimension=0, tiled=True)  67.7 us
    unnamed x298, local copies, waits for them, and re-layouts  60.6 us
    unnamed x2, blocking collectives  50.7 us
    dot_general x32, matrix products, block_step(): jnp.einsum('in,hpn->ihp', c_blk, carried_state, precision=HIGHEST_PRECISION)  48.3 us
  transfers between devices with their start and end apart: 19, of which 9 were waited for; matrix products, arithmetic and copies ran while one was open for 49% of the time, Pallas kernels for 0%

commit v1 on v0

--- a/solution.py
+++ b/solution.py
@@ -58,7 +58,11 @@
     def block_step(carry, item):
         carried_state, last_seg = carry
         x_blk, dt_blk, b_blk, c_blk, seg_blk = item
-        logs = jnp.cumsum(dt_blk * rates[None, :], axis=0)
+        logs = jnp.dot(
+            (rows_iota >= cols_iota).astype(jnp.float32),
+            dt_blk * rates[None, :],
+            precision=HIGHEST_PRECISION,
+        )
         inside = (rows_iota >= cols_iota) & (seg_blk[:, None] == seg_blk[None, :])
         logs_t = logs.T
         diffs = jnp.where(inside[None], logs_t[:, :, None] - logs_t[:, None, :], -jnp.inf)

time: 1610 us -> 1360 us (0.84)
  other arithmetic: 366 us -> 180 us
  local copies, waits for them, and re-layouts: 554 us -> 460 us
  matrix products: 264 us -> 293 us
    another operation x64 -> x0, other arithmetic: 144 us -> none
    another operation x129 -> x17, local copies, waits for them, and re-layouts: 103 us -> 13.1 us
    dot_general x0 -> x24, matrix products: none -> 29.2 us  [block_step(): jnp.dot((rows_iota >= cols_iota).astype(jnp.float32), dt_blk * rates[None...]
  transfers between devices with their start and end apart: 19 -> 19, of which waited for: 9 -> 9; matrix products, arithmetic and copies ran while one was open for 49% -> 48% of each run, Pallas kernels for 0% -> 0%
where the time goes in v1:
time: 1360 us; the launch traced here: 1340 us
  local copies, waits for them, and re-layouts  460 us (34%)
  matrix products  293 us (22%)
  other arithmetic  180 us (13%)
  blocking collectives  161 us (12%)
  waiting for transfers between devices  151 us (11%)
  starting transfers between devices  49.6 us (4%)
  loops' own time  22.7 us (2%)
  between operations  20.1 us (1%)
    dynamic_update_slice x40, local copies, waits for them, and re-layouts, scan_blocks(): lax.scan(jax.checkpoint(block_step), (start_state, jnp.int32(-1)), (x_blo...  181 us
    dot_general x24, matrix products, block_step(): jnp.einsum('hij,jhp->ihp', weights, x_blk, precision=HIGHEST_PRECISION)  81.2 us
    reduce_scatter x1, waiting for transfers between devices, on_device(): lax.psum_scatter(grad_in_mat, 'fsdp', scatter_dimension=0, tiled=True)  67.8 us
    unnamed x298, local copies, waits for them, and re-layouts  60.5 us
    dot_general x32, matrix products, block_step(): jnp.einsum('in,hpn->ihp', c_blk, carried_state, precision=HIGHEST_PRECISION)  55.5 us
    squeeze x32, local copies, waits for them, and re-layouts, scan_blocks(): lax.scan(jax.checkpoint(block_step), (start_state, jnp.int32(-1)), (x_blo...  52.3 us
    unnamed x2, blocking collectives  50.7 us
    all_gather x2, blocking collectives, on_device(): bc_whole = lax.all_gather(bc_send, 'seq', axis=0, tiled=True)  41 us
  transfers between devices with their start and end apart: 19, of which 9 were waited for; matrix products, arithmetic and copies ran while one was open for 48% of the time, Pallas kernels for 0%

profile of v1, /device:TPU:0, one launch (start us, length us, event | category | flops | bytes accessed | tf_op | source)
XLA Modules:
  0.0 1338.2 jit_solution(8534494571511180450)
XLA Ops:
  16.9 26.0 %all-reduce.62 = (bf16[768]{0:T(1024)(128)(2,1)S(1)}, bf16[1792]{0:T(1024)(128)(2,1)S(1)}, bf16[1536]{0:T(1024)(128)(2,1)}) all-reduce(bf16[768]{0:T(1024)(128)(2,1)S(1)} %dynamic-update-slice, bf16[1792]{0:T(1024)(128)(2,1)S(1)} %dynamic-update-slice.1, ...), channel_id=1, replica_groups=mesh['fsdp'=8,'seq'=4] {'fsdp'}, use_global_device_ids=true, to_apply=%add.52 | all-reduce | flops 4096 | bytes 16384
  94.8 24.8 %all_gather.28 = bf16[1024,256]{0,1:T(8,128)(2,1)S(1)} all-gather(bf16[256,256]{0,1:T(8,128)(2,1)S(1)} %slice.316), channel_id=1, replica_groups=mesh['fsdp'=8,'seq'=4] {'seq'}, dimensions={0}, use_global_device_ids=true | all-gather | bytes 655360 | tf_op jit(solution)/shard_map/all_gather | solution.py:177
  122.0 16.2 %all_gather.31 = bf16[1024,256]{0,1:T(8,128)(2,1)S(1)} all-gather(bf16[256,256]{0,1:T(8,128)(2,1)S(1)} %slice.331), channel_id=1, replica_groups=mesh['fsdp'=8,'seq'=4] {'seq'}, dimensions={0}, use_global_device_ids=true | all-gather | bytes 655360 | tf_op jit(solution)/shard_map/all_gather | solution.py:177
  178.3 111.0 %while.91 = (s32[]{:T(128)}, f32[6,64,128]{2,1,0:T(8,128)S(1)}, s32[]{:T(128)}, f32[4,256,6,64]{1,0,3,2:T(4,128)}, f32[4,6,64,128]{3,2,1,0:T(8,128)}, /*index=5*...) while((s32[]{:T(128)}, f32[6,64,128]{2,1,0:T(8,128)S(1)}, ...), condition=%wide.region_6.8_spmd.clone, body=%wide.region_5.7_spmd.clone.sunk | while | flops 711811584 | bytes 5827731 | solution.py:86
  191.7 9.6 dynamic_update_slice.172
  219.4 9.6 dynamic_update_slice.172
  247.1 9.6 dynamic_update_slice.172
  274.8 9.6 dynamic_update_slice.172
  297.9 104.3 %while.90 = (s32[]{:T(128)}, f32[6,64,128]{2,1,0:T(8,128)S(1)}, s32[]{:T(128)}, f32[4,256,6,64]{1,0,3,2:T(4,128)}, f32[4,6,64,128]{3,2,1,0:T(8,128)}, /*index=5*...) while((s32[]{:T(128)}, f32[6,64,128]{2,1,0:T(8,128)S(1)}, ...), condition=%wide.region_2.4_spmd.clone, body=%wide.region_1.3_spmd.clone.sunk | while | flops 711811584 | bytes 5801883 | solution.py:86
  309.6 9.5 dynamic_update_slice.169
  335.7 9.5 dynamic_update_slice.169
  361.8 9.5 dynamic_update_slice.169
  387.8 9.5 dynamic_update_slice.169
  497.9 11.0 all-to-all-done.9
  519.3 225.7 %while.93 = (s32[]{:T(128)}, f32[6]{0:T(128)}, f32[6,64,128]{2,1,0:T(8,128)}, f32[4,256,6,64]{1,0,3,2:T(4,128)}, f32[4,256,6]{1,2,0:T(8,128)}, /*index=5*/f32[4,...) while((s32[]{:T(128)}, f32[6]{0:T(128)}, ...), condition=%wide.region_31.33_spmd.clone, body=%wide.region_22.32_spmd.clone.sunk | while | flops 1678432768 | bytes 21140992 | solution.py:86
  562.3 9.5 dynamic_update_slice.181
  618.4 9.5 dynamic_update_slice.181
  675.2 9.5 dynamic_update_slice.181
  757.4 226.3 %while.92 = (s32[]{:T(128)}, f32[6]{0:T(128)}, f32[6,64,128]{2,1,0:T(8,128)}, f32[4,256,6,64]{1,0,3,2:T(4,128)}, f32[4,256,6]{1,2,0:T(8,128)}, /*index=5*/f32[4,...) while((s32[]{:T(128)}, f32[6]{0:T(128)}, ...), condition=%wide.region_18.20_spmd.clone, body=%wide.region_9.19_spmd.clone.sunk | while | flops 1678432768 | bytes 21140992 | solution.py:86
  800.5 9.5 dynamic_update_slice.177
  856.9 9.5 dynamic_update_slice.177
  913.8 9.5 dynamic_update_slice.177
  970.8 9.5 dynamic_update_slice.177
  1047.3 10.5 all_to_all.148
  1075.0 11.0 all-to-all-done.7
  1097.0 9.5 all-to-all-done.10
  1119.0 10.2 convolution_add_fusion.8
  1136.7 37.8 %all-reduce.58 = (f32[24]{0:T(128)}, f32[24]{0:T(128)}, f32[24]{0:T(128)}) all-reduce(f32[24]{0:T(128)S(1)} %add_dynamic-update-slice_fusion.3, f32[24]{0:T(128)S(1)} %multiply_dynamic-update-slice_fusion, f32[24]{0:T(128)S(1)} %add_dynamic-update-slice_fusion.2), channel_id=1, replica_groups=mesh['fsdp'=8,'seq'=4] {'fsdp','seq'}, use_global_device_ids=true, to_apply=%region_66.68 | all-reduce | flops 72 | bytes 576 | tf_op jit(solution)/shard_map/psum | solution.py:284
  1175.9 67.8 %reduce-scatter.12.cloned.1.call-done = f32[96,3352]{1,0:T(8,128)} async-done(((f32[768,3352]{1,0:T(8,128)}), f32[96,3352]{1,0:T(8,128)}) %reduce-scatter.12.cloned.1.call-update) | async-done | bytes 1287184 | tf_op jit(solution)/shard_map/reduce_scatter | solution.py:275
  1251.5 24.7 %all-reduce.59 = (f32[768]{0:T(1024)S(1)}, f32[1792]{0:T(1024)S(1)}, f32[1536]{0:T(1024)S(1)}) all-reduce(f32[768]{0:T(1024)S(1)} %add.448, f32[1792]{0:T(1024)S(1)} %pad_maximum_fusion.7, f32[1536]{0:T(1024)S(1)} %add.458), channel_id=4, replica_groups=mesh['fsdp'=8,'seq'=4] {'fsdp'}, use_global_device_ids=true, to_apply=%region_36.38.clone | all-reduce | flops 4096 | bytes 32768
  1276.3 13.0 all-reduce.60
  1292.9 34.9 %all-reduce.65.cloned.1.call-done = (f32[96,3352]{1,0:T(8,128)}, f32[192,768]{1,0:T(8,128)}) async-done(((f32[96,3352]{1,0:T(8,128)}, f32[192,768]{1,0:T(8,128)}), (f32[96,3352]{1,0:T(8,128)}, f32[192,768]{1,0:T(8,128)})) %all-reduce.65.cloned.1.call-update) | async-done | bytes 1877008 | tf_op jit(solution)/shard_map/psum | solution.py:281
  (1158 shorter events, 855.0 us)
Async XLA Ops:
  7.2 35.7 %copy-start.20 = (bf16[1,2,256,768]{3,2,1,0:T(8,128)(2,1)S(1)}, bf16[1,2,256,768]{3,2,1,0:T(8,128)(2,1)}, u32[]{:S(2)}) copy-start(bf16[1,2,256,768]{3,2,1,0:T(8,128)(2,1)} %param.21) | copy-start | bytes 2359300
  7.2 36.0 %copy-start.154 = (bf16[224,4]{0,1:T(4,128)(2,1)S(1)}, bf16[224,4]{0,1:T(4,128)(2,1)}, u32[]{:S(2)}) copy-start(bf16[224,4]{0,1:T(4,128)(2,1)} %param.25) | copy-start | bytes 5380
  7.2 47.1 %all-gather.4.cloned.1.call-start = ((), (), s32[]{:S(2)}) async-start(), calls=%async_computation.17 | async-start | bytes 5971968 | tf_op jit(solution)/shard_map/all_gather | solution.py:126
  7.9 437.8 %all-gather.6.cloned.1.call-start = ((), (), s32[]{:S(2)}) async-start(), calls=%async_computation.18 | async-start | bytes 2654208 | tf_op jit(solution)/shard_map/all_gather | solution.py:132
  61.5 13.0 all-to-all-start
  74.5 11.1 all-to-all-start.3
  85.6 56.1 %all-to-all-start.1 = ((bf16[256,24,64]{0,2,1:T(8,128)(2,1)}), bf16[256,24,64]{0,2,1:T(8,128)(2,1)}, u32[]{:S(2)}, u32[]{:S(2)}) async-start(bf16[256,24,64]{0,2,1:T(8,128)(2,1)} %bitcast.9), calls=%async_computation.1 | async-start | bytes 1572864 | tf_op jit(solution)/shard_map/all_to_all | solution.py:179
  92.0 72.5 %copy-start.100 = (f32[1024]{0:T(1024)}, f32[1024]{0:T(1024)S(1)}, u32[]{:S(2)}) copy-start(f32[1024]{0:T(1024)S(1)} %get-tuple-element.1856) | copy-start | bytes 12292
  92.0 72.5 %copy-start.102 = (f32[1024]{0:T(1024)}, f32[1024]{0:T(1024)S(1)}, u32[]{:S(2)}) copy-start(f32[1024]{0:T(1024)S(1)} %get-tuple-element.1858) | copy-start | bytes 12292
  92.7 71.9 %copy-start.104 = (f32[1024]{0:T(1024)}, f32[1024]{0:T(1024)S(1)}, u32[]{:S(2)}) copy-start(f32[1024]{0:T(1024)S(1)} %get-tuple-element.1859) | copy-start | bytes 12292
  92.7 71.9 %copy-start.106 = (f32[1024]{0:T(1024)}, f32[1024]{0:T(1024)S(1)}, u32[]{:S(2)}) copy-start(f32[1024]{0:T(1024)S(1)} %get-tuple-element.1861) | copy-start | bytes 12292
  119.6 26.8 %copy-start.14 = (bf16[1024,256]{0,1:T(8,128)(2,1)}, bf16[1024,256]{0,1:T(8,128)(2,1)S(1)}, u32[]{:S(2)}) copy-start(bf16[1024,256]{0,1:T(8,128)(2,1)S(1)} %all_gather.28) | copy-start | bytes 1572868
  119.7 26.7 %copy-start.33 = (f32[1023,256]{0,1:T(8,128)}, f32[1023,256]{0,1:T(8,128)S(1)}, u32[]{:S(2)}) copy-start(f32[1023,256]{0,1:T(8,128)S(1)} %slice.318) | copy-start | bytes 3142660
  141.6 20.2 %all-to-all-start.4 = ((bf16[256,24,64]{0,2,1:T(8,128)(2,1)}), bf16[256,24,64]{0,2,1:T(8,128)(2,1)}, u32[]{:S(2)}, u32[]{:S(2)}) async-start(bf16[256,24,64]{0,2,1:T(8,128)(2,1)} %bitcast.730), calls=%async_computation.4 | async-start | bytes 1572864 | tf_op jit(solution)/shard_map/all_to_all | solution.py:179
  420.7 20.8 %all-to-all-start.2 = ((bf16[4,2,49152]{2,1,0:T(2,128)(2,1)}), bf16[4,2,49152]{2,1,0:T(2,128)(2,1)}, u32[]{:S(2)}, u32[]{:S(2)}) async-start(bf16[4,2,49152]{2,1,0:T(2,128)(2,1)} %reshape.781), calls=%async_computation.2 | async-start | bytes 1572864 | tf_op jit(solution)/shard_map/all_to_all | solution.py:196
  441.5 23.5 %all-to-all-start.5 = ((bf16[4,2,49152]{2,1,0:T(2,128)(2,1)}), bf16[4,2,49152]{2,1,0:T(2,128)(2,1)}, u32[]{:S(2)}, u32[]{:S(2)}) async-start(bf16[4,2,49152]{2,1,0:T(2,128)(2,1)} %reshape.779), calls=%async_computation.5 | async-start | bytes 1572864 | tf_op jit(solution)/shard_map/all_to_all | solution.py:196
  445.7 47.7 %copy-start.84 = (f32[1536]{0:T(1024)}, f32[1536]{0:T(1024)S(1)}, u32[]{:S(2)}) copy-start(f32[1536]{0:T(1024)S(1)} %convert_element_type.375) | copy-start | bytes 18436
  464.9 28.5 %copy-start.124 = (f32[256]{0:T(256)}, f32[256]{0:T(256)S(1)}, u32[]{:S(2)}) copy-start(f32[256]{0:T(256)S(1)} %fusion.303) | copy-start | bytes 3076
  486.3 22.5 %all-to-all-start.9 = ((bf16[256,24,64]{0,2,1:T(8,128)(2,1)}), bf16[256,24,64]{0,2,1:T(8,128)(2,1)}, u32[]{:S(2)}, u32[]{:S(2)}) async-start(bf16[256,24,64]{0,2,1:T(8,128)(2,1)} %bitcast.725), calls=%async_computation.10 | async-start | bytes 1572864 | tf_op jit(solution)/shard_map/all_to_all | solution.py:211
  508.9 241.4 %all-to-all-start.6 = ((bf16[256,24,64]{0,2,1:T(8,128)(2,1)}), bf16[256,24,64]{0,2,1:T(8,128)(2,1)}, u32[]{:S(2)}, u32[]{:S(2)}) async-start(bf16[256,24,64]{0,2,1:T(8,128)(2,1)} %bitcast.722), calls=%async_computation.6 | async-start | bytes 1572864 | tf_op jit(solution)/shard_map/all_to_all | solution.py:211
  513.1 598.4 %reduce-scatter.8.cloned.1.call-start = ((), (), s32[]{:S(2)}) async-start(), calls=%async_computation.19 | async-start | bytes 655360 | tf_op jit(solution)/shard_map/reduce_scatter | solution.py:232
  1017.8 101.1 %reduce-scatter.10.cloned.1.call-start = ((), (), s32[]{:S(2)}) async-start(), calls=%async_computation.20 | async-start | bytes 655360 | tf_op jit(solution)/shard_map/reduce_scatter | solution.py:232
  1032.2 142.7 %reduce-scatter.16.cloned.1.call-start = ((), (), s32[]{:S(2)}) async-start(), calls=%async_computation.23 | async-start | bytes 1032192
  1040.2 135.7 %reduce-scatter.14.cloned.1.call-start = ((), (), s32[]{:S(2)}) async-start(), calls=%async_computation.22 | async-start | bytes 5308416 | tf_op jit(solution)/shard_map/reduce_scatter | solution.py:279
  1057.8 8.8 all-to-all-start.11
  1066.6 19.4 %all-to-all-start.7 = ((bf16[4,2,49152]{2,1,0:T(2,128)(2,1)}), bf16[4,2,49152]{2,1,0:T(2,128)(2,1)}, u32[]{:S(2)}, u32[]{:S(2)}) async-start(bf16[4,2,49152]{2,1,0:T(2,128)(2,1)} %reshape.785), calls=%async_computation.7 | async-start | bytes 1572864 | tf_op jit(solution)/shard_map/all_to_all | solution.py:221
  1086.0 20.5 %all-to-all-start.10 = ((bf16[4,2,49152]{2,1,0:T(2,128)(2,1)}), bf16[4,2,49152]{2,1,0:T(2,128)(2,1)S(1)}, u32[]{:S(2)}, u32[]{:S(2)}) async-start(bf16[4,2,49152]{2,1,0:T(2,128)(2,1)} %reshape.783), calls=%async_computation.11 | async-start | bytes 1572864 | tf_op jit(solution)/shard_map/all_to_all | solution.py:221
  1089.5 154.1 %reduce-scatter.12.cloned.1.call-start = ((), (), s32[]{:S(2)}) async-start(), calls=%async_computation.21 | async-start | bytes 11943936 | tf_op jit(solution)/shard_map/reduce_scatter | solution.py:275
  1129.2 198.6 %all-reduce.65.cloned.1.call-start = ((), (), s32[]{:S(2)}) async-start(), calls=%async_computation.24 | async-start | bytes 3833856 | tf_op jit(solution)/shard_map/psum | solution.py:281
  1133.9 114.7 %slice-start = ((s8[5308416]{0:T(1024)(128)(4,1)}), s8[1114112]{0:T(1024)(128)(4,1)S(1)}, s32[]{:S(2)}) async-start(s8[5308416]{0:T(1024)(128)(4,1)} %bitcast.692), calls=%async_computation.25 | async-start | bytes 2228224
  1248.7 40.7 %copy-start.145 = (f32[256]{0:T(256)S(1)}, f32[256]{0:T(256)}, u32[]{:S(2)}) copy-start(f32[256]{0:T(256)} %copy-done.144) | copy-start | bytes 3076
  1248.7 40.7 %copy-start.147 = (f32[256]{0:T(256)S(1)}, f32[256]{0:T(256)}, u32[]{:S(2)}) copy-start(f32[256]{0:T(256)} %copy-done.146) | copy-start | bytes 3076
  (243 other events, 1369.7 us)
Sparse Core Ops, SparseCore 0:
  9.9 44.3 all-gather.3
  56.2 28.9 all-gather.5
  1018.0 22.0 reduce-scatter.7
  1042.7 20.0 reduce-scatter.9
  1066.4 33.6 reduce-scatter.15
  1103.4 54.2 reduce-scatter.13
  1161.5 82.0 reduce-scatter.11
  1246.3 81.4 all-reduce.64
